TPU v7x, 32 devices: a whole 2x2x4 slice. The times are simulated.
32 devices in a mesh: dcn: 4 (over y, x), ctx: 4 (over z), head: 2 (over core).
Axes of the slice: x: 2, y: 2, z: 4, core: 2. Of those that a mesh axis runs over, the one named last changes fastest.
Arguments:
- queries: bfloat16 [4096, 64, 128], P(('dcn', 'ctx'), 'head'), may hold values from -26 to 26
- keys: bfloat16 [4096, 8, 128], P(('dcn', 'ctx'), 'head'), may hold values from -6 to 6
- values: bfloat16 [4096, 8, 128], P(('dcn', 'ctx'), 'head'), may hold values from -6 to 6
- seg_ids: int32 [4096], P(('dcn', 'ctx')), may hold values from 0 to 15, never falling along the last dimension, each value on 1 to 768 neighbouring positions
Outputs:
- attended: bfloat16 [4096, 64, 128], P(('dcn', 'ctx'), 'head')
Inputs may be any that keep to these rules, and one draw needn't show every extreme that they name: `seg_ids`: ids never fall along the sequence; every document has 1 to 768 tokens and one has exactly 768.
All inputs are finite; a program needn't handle non-finite values.
Results may differ from a plain program's by a relative error of at most 0.0025.
Values may be sent and summed in bfloat16 or wider, within the bound.
A program may use at most 64 MiB of HBM per device.

v0:
```python
import jax
import jax.numpy as jnp
from jax import lax
from jax.sharding import PartitionSpec as P

STEPS = 3


def passed_along(x, axis, by):
    count = lax.axis_size(axis)
    pairs = [(i, i + by) for i in range(count) if 0 <= i + by < count]
    return lax.ppermute(x, axis, pairs)


def local(queries, keys, values, seg_ids):
    tok_rows = queries.shape[0]
    kv_local = keys.shape[1]
    head_dim = queries.shape[2]
    group_size = queries.shape[1] // kv_local
    position = lax.axis_index(("dcn", "ctx"))
    query_pos = position * tok_rows + jnp.arange(tok_rows, dtype=jnp.int32)
    grouped = queries.reshape(tok_rows, kv_local, group_size, head_dim)
    factor = head_dim ** (-0.5)

    def attend(state, key_tile, val_tile, key_seg, key_start):
        key_pos = key_start + jnp.arange(key_tile.shape[0], dtype=jnp.int32)
        mask = (
            (seg_ids[:, None] == key_seg[None, :])
            & (key_pos[None, :] <= query_pos[:, None])
            & (key_pos[None, :] >= 0)
        )
        run_max, run_sum, weighted = state
        scores = (
            jnp.einsum("qkgd,skd->kgqs", grouped, key_tile, preferred_element_type=jnp.float32)
            * factor
        )
        scores = jnp.where(mask, scores, -1e30)
        new_max = jnp.maximum(run_max, jnp.max(scores, axis=-1))
        weights = jnp.where(mask, jnp.exp(scores - new_max[..., None]), 0.0)
        rescale = jnp.exp(run_max - new_max)
        new_sum = run_sum * rescale + jnp.sum(weights, axis=-1)
        update = jnp.einsum(
            "kgqs,skd->kgqd",
            weights.astype(jnp.bfloat16),
            val_tile,
            preferred_element_type=jnp.float32,
        )
        return (new_max, new_sum, weighted * rescale[..., None] + update)

    state = (
        jnp.full((kv_local, group_size, tok_rows), -1e30, jnp.float32),
        jnp.zeros((kv_local, group_size, tok_rows), jnp.float32),
        jnp.zeros((kv_local, group_size, tok_rows, head_dim), jnp.float32),
    )
    state = attend(state, keys, values, seg_ids, position * tok_rows)

    def advance(distance, carry):
        current, carried = carry
        carried = passed_along((carried[0], carried[1], carried[2]), ("dcn", "ctx"), 1)
        current = attend(
            current, carried[0], carried[1], carried[2], (position - distance) * tok_rows
        )
        return (current, carried)

    state, _ = lax.fori_loop(1, STEPS + 1, advance, (state, (keys, values, seg_ids)))
    run_max, run_sum, weighted = state
    result = weighted / run_sum[..., None]
    return (
        result.transpose(2, 0, 1, 3)
        .reshape(tok_rows, kv_local * group_size, head_dim)
        .astype(jnp.bfloat16)
    )


def solution(mesh):
    placed = (
        P(("dcn", "ctx"), "head", None),
        P(("dcn", "ctx"), "head", None),
        P(("dcn", "ctx"), "head", None),
        P(("dcn", "ctx")),
    )
    return jax.shard_map(
        local,
        mesh=mesh,
        in_specs=placed,
        out_specs=P(("dcn", "ctx"), "head", None),
        check_vma=False,
    )
```

profile of v0, /device:TPU:4, one launch (start us, length us, event | category | flops | bytes accessed | tf_op | source)
XLA Modules:
  0.0 97.6 jit_solution(74102203931283179)
XLA Ops:
  0.9 2.4 %copy.6 = bf16[256,32,128]{2,0,1:T(8,128)(2,1)S(1)} copy(bf16[256,32,128]{2,1,0:T(8,128)(2,1)} %param.6) | data formatting | bytes 4194304 | tf_op args[0]
  3.3 2.3 %fusion.20 = (f32[4,8,256]{2,1,0:T(8,128)S(1)}, f32[4,256,256,8]{2,1,3,0:T(8,128)S(1)}) fusion(pred[256,256]{0,1:T(8,128)(4,1)S(1)} %and_and_fusion.1, bf16[256,4,8,128]{3,0,2,1:T(8,128)(2,1)S(1)} %bitcast.60, bf16[256,4,128,1]{2,1,0,3:T(4,128)(2,1)} %bitcast.62), kind=kOutput, calls=%fused_computation.27 | convolution fusion | flops 543154176 | bytes 10846208 | tf_op jit(solution)/shard_map/qkgd,skd->kgqs/dot_general | solution.py:34
  5.7 2.1 %fusion.22 = f32[4,8,256]{2,1,0:T(8,128)S(1)} fusion(f32[4,256,256,8]{2,1,3,0:T(8,128)S(1)} %get-tuple-element.259, f32[4,8,256]{2,1,0:T(8,128)S(1)} %broadcast_maximum_fusion, pred[256,256]{0,1:T(8,128)(4,1)S(1)} %and_and_fusion.1), kind=kLoop, calls=%fused_computation.29 | loop fusion | flops 10477568 | bytes 8519680 | tf_op jit(solution)/shard_map/reduce_sum | solution.py:41
  7.9 4.8 %broadcast_add_fusion = f32[4,8,256,128]{3,2,1,0:T(8,128)} fusion(f32[4,8,256]{2,1,0:T(8,128)S(1)} %get-tuple-element.256, f32[4,256,256,8]{2,1,3,0:T(8,128)S(1)} %get-tuple-element.259, f32[4,8,256]{2,1,0:T(8,128)S(1)} %broadcast_maximum_fusion, pred[256,256]{0,1:T(8,128)(4,1)S(1)} %and_and_fusion.1, bf16[256,4,128,1]{2,1,0,3:T(4,128)(2,1)S(1)} %bitcast.63), kind=kOutput, calls=%fused_computation.38 | convolution fusion | flops 548405248 | bytes 12976128 | tf_op jit(solution)/shard_map/kgqs,skd->kgqd/dot_general | solution.py:42
  12.8 79.2 %while.24 = (s32[]{:T(128)}, f32[4,8,256]{2,1,0:T(8,128)S(1)}, f32[4,8,256]{2,1,0:T(8,128)S(1)}, f32[4,8,256,128]{3,2,1,0:T(8,128)}, bf16[256,4,128]{2,0,1:T(8,1...) while((s32[]{:T(128)}, f32[4,8,256]{2,1,0:T(8,128)S(1)}, ...), condition=%wide.region_5.6_spmd.clone, body=%wide.region_2.5_spmd.clone.sunk | while | flops 1103381504 | bytes 73675600 | solution.py:65
  12.8 3.5 %collective-permute-start = (s32[256]{0:T(256)S(1)}, s32[256]{0:T(256)S(1)}, u32[]{:S(2)}, u32[]{:S(2)}) collective-permute-start(s32[256]{0:T(256)S(1)} %get-tuple-element.358), channel_id=1, source_target_pairs={{0,2},{2,4},{4,6},{6,8},{8,10},{10,12},{12,14},{14,16},{16,18},{18... | collective-permute-start | bytes 3080 | tf_op jit(solution)/shard_map/while/body/eval_jaxpr/ppermute | solution.py:12
  16.3 3.5 %collective-permute-start.1 = (bf16[256,4,128]{2,0,1:T(8,128)(2,1)S(1)}, bf16[256,4,128]{2,0,1:T(8,128)(2,1)S(1)}, u32[]{:S(2)}, u32[]{:S(2)}) collective-permute-start(bf16[256,4,128]{2,0,1:T(8,128)(2,1)S(1)} %get-tuple-element.356), channel_id=1, source_target_pairs={{0,2},{2,4},{4,6},{6,8},{8,10},{10,12},{12,14},{14,16},{16,18},{18... | collective-permute-start | bytes 786440 | tf_op jit(solution)/shard_map/while/body/eval_jaxpr/ppermute | solution.py:12
  19.8 3.5 %collective-permute-start.2 = (bf16[256,4,128]{2,0,1:T(8,128)(2,1)S(1)}, bf16[256,4,128]{2,0,1:T(8,128)(2,1)S(1)}, u32[]{:S(2)}, u32[]{:S(2)}) collective-permute-start(bf16[256,4,128]{2,0,1:T(8,128)(2,1)S(1)} %get-tuple-element.357), channel_id=1, source_target_pairs={{0,2},{2,4},{4,6},{6,8},{8,10},{10,12},{12,14},{14,16},{16,18},{18... | collective-permute-start | bytes 786440 | tf_op jit(solution)/shard_map/while/body/eval_jaxpr/ppermute | solution.py:12
  23.5 7.5 %collective-permute-done.1 = bf16[256,4,128]{2,0,1:T(8,128)(2,1)S(1)} collective-permute-done((bf16[256,4,128]{2,0,1:T(8,128)(2,1)S(1)}, bf16[256,4,128]{2,0,1:T(8,128)(2,1)S(1)}, u32[]{:S(2)}, u32[]{:S(2)}) %collective-permute-start.1) | collective-permute-done | bytes 262176 | tf_op jit(solution)/shard_map/while/body/eval_jaxpr/ppermute | solution.py:12
  32.4 2.1 %fusion.51 = f32[4,8,256]{2,1,0:T(8,128)S(1)} fusion(f32[4,256,256,8]{2,1,3,0:T(8,128)S(1)} %get-tuple-element.336, f32[4,8,256]{2,1,0:T(8,128)S(1)} %max.9, pred[256,256]{0,1:T(8,128)(4,1)S(1)} %and_and_fusion.3), kind=kLoop, calls=%fused_computation.5.clone.1 | loop fusion | flops 10477568 | bytes 8519680 | tf_op jit(solution)/shard_map/while/body/eval_jaxpr/reduce_sum | solution.py:41
  35.2 3.8 %multiply_add_fusion.5 = f32[4,8,256,128]{3,2,1,0:T(8,128)S(1)} fusion(f32[4,8,256,128]{3,2,1,0:T(8,128)S(1)} %copy-done, f32[4,8,256]{2,1,0:T(8,128)S(1)} %get-tuple-element.338, f32[4,256,256,8]{2,1,3,0:T(8,128)S(1)} %get-tuple-element.336, f32[4,8,256]{2,1,0:T(8,128)S(1)} %max.9, pred[256,256]{0,1:T(8,128)(4,1)S(1)} %and_and_fusion.3, ...), kind=kOutput, calls=%fused_computation.7.clone.1 | convolution fusion | flops 549453824 | bytes 17170432 | tf_op jit(solution)/shard_map/while/body/eval_jaxpr/kgqs,skd->kgqd/dot_general | solution.py:42
  44.8 2.6 %collective-permute-start.2 = (bf16[256,4,128]{2,0,1:T(8,128)(2,1)S(1)}, bf16[256,4,128]{2,0,1:T(8,128)(2,1)S(1)}, u32[]{:S(2)}, u32[]{:S(2)}) collective-permute-start(bf16[256,4,128]{2,0,1:T(8,128)(2,1)S(1)} %get-tuple-element.357), channel_id=1, source_target_pairs={{0,2},{2,4},{4,6},{6,8},{8,10},{10,12},{12,14},{14,16},{16,18},{18... | collective-permute-start | bytes 786440 | tf_op jit(solution)/shard_map/while/body/eval_jaxpr/ppermute | solution.py:12
  47.4 2.6 %collective-permute-done = s32[256]{0:T(256)S(1)} collective-permute-done((s32[256]{0:T(256)S(1)}, s32[256]{0:T(256)S(1)}, u32[]{:S(2)}, u32[]{:S(2)}) %collective-permute-start) | collective-permute-done | bytes 1056 | tf_op jit(solution)/shard_map/while/body/eval_jaxpr/ppermute | solution.py:12
  50.1 7.4 %collective-permute-done.1 = bf16[256,4,128]{2,0,1:T(8,128)(2,1)S(1)} collective-permute-done((bf16[256,4,128]{2,0,1:T(8,128)(2,1)S(1)}, bf16[256,4,128]{2,0,1:T(8,128)(2,1)S(1)}, u32[]{:S(2)}, u32[]{:S(2)}) %collective-permute-start.1) | collective-permute-done | bytes 262176 | tf_op jit(solution)/shard_map/while/body/eval_jaxpr/ppermute | solution.py:12
  58.9 2.1 %fusion.51 = f32[4,8,256]{2,1,0:T(8,128)S(1)} fusion(f32[4,256,256,8]{2,1,3,0:T(8,128)S(1)} %get-tuple-element.336, f32[4,8,256]{2,1,0:T(8,128)S(1)} %max.9, pred[256,256]{0,1:T(8,128)(4,1)S(1)} %and_and_fusion.3), kind=kLoop, calls=%fused_computation.5.clone.1 | loop fusion | flops 10477568 | bytes 8519680 | tf_op jit(solution)/shard_map/while/body/eval_jaxpr/reduce_sum | solution.py:41
  61.2 3.8 %multiply_add_fusion.5 = f32[4,8,256,128]{3,2,1,0:T(8,128)S(1)} fusion(f32[4,8,256,128]{3,2,1,0:T(8,128)S(1)} %copy-done, f32[4,8,256]{2,1,0:T(8,128)S(1)} %get-tuple-element.338, f32[4,256,256,8]{2,1,3,0:T(8,128)S(1)} %get-tuple-element.336, f32[4,8,256]{2,1,0:T(8,128)S(1)} %max.9, pred[256,256]{0,1:T(8,128)(4,1)S(1)} %and_and_fusion.3, ...), kind=kOutput, calls=%fused_computation.7.clone.1 | convolution fusion | flops 549453824 | bytes 17170432 | tf_op jit(solution)/shard_map/while/body/eval_jaxpr/kgqs,skd->kgqd/dot_general | solution.py:42
  70.7 3.3 %collective-permute-start.2 = (bf16[256,4,128]{2,0,1:T(8,128)(2,1)S(1)}, bf16[256,4,128]{2,0,1:T(8,128)(2,1)S(1)}, u32[]{:S(2)}, u32[]{:S(2)}) collective-permute-start(bf16[256,4,128]{2,0,1:T(8,128)(2,1)S(1)} %get-tuple-element.357), channel_id=1, source_target_pairs={{0,2},{2,4},{4,6},{6,8},{8,10},{10,12},{12,14},{14,16},{16,18},{18... | collective-permute-start | bytes 786440 | tf_op jit(solution)/shard_map/while/body/eval_jaxpr/ppermute | solution.py:12
  74.0 2.0 %collective-permute-done = s32[256]{0:T(256)S(1)} collective-permute-done((s32[256]{0:T(256)S(1)}, s32[256]{0:T(256)S(1)}, u32[]{:S(2)}, u32[]{:S(2)}) %collective-permute-start) | collective-permute-done | bytes 1056 | tf_op jit(solution)/shard_map/while/body/eval_jaxpr/ppermute | solution.py:12
  76.2 6.5 %collective-permute-done.1 = bf16[256,4,128]{2,0,1:T(8,128)(2,1)S(1)} collective-permute-done((bf16[256,4,128]{2,0,1:T(8,128)(2,1)S(1)}, bf16[256,4,128]{2,0,1:T(8,128)(2,1)S(1)}, u32[]{:S(2)}, u32[]{:S(2)}) %collective-permute-start.1) | collective-permute-done | bytes 262176 | tf_op jit(solution)/shard_map/while/body/eval_jaxpr/ppermute | solution.py:12
  84.1 2.1 %fusion.51 = f32[4,8,256]{2,1,0:T(8,128)S(1)} fusion(f32[4,256,256,8]{2,1,3,0:T(8,128)S(1)} %get-tuple-element.336, f32[4,8,256]{2,1,0:T(8,128)S(1)} %max.9, pred[256,256]{0,1:T(8,128)(4,1)S(1)} %and_and_fusion.3), kind=kLoop, calls=%fused_computation.5.clone.1 | loop fusion | flops 10477568 | bytes 8519680 | tf_op jit(solution)/shard_map/while/body/eval_jaxpr/reduce_sum | solution.py:41
  86.3 3.8 %multiply_add_fusion.5 = f32[4,8,256,128]{3,2,1,0:T(8,128)S(1)} fusion(f32[4,8,256,128]{3,2,1,0:T(8,128)S(1)} %copy-done, f32[4,8,256]{2,1,0:T(8,128)S(1)} %get-tuple-element.338, f32[4,256,256,8]{2,1,3,0:T(8,128)S(1)} %get-tuple-element.336, f32[4,8,256]{2,1,0:T(8,128)S(1)} %max.9, pred[256,256]{0,1:T(8,128)(4,1)S(1)} %and_and_fusion.3, ...), kind=kOutput, calls=%fused_computation.7.clone.1 | convolution fusion | flops 549453824 | bytes 17170432 | tf_op jit(solution)/shard_map/while/body/eval_jaxpr/kgqs,skd->kgqd/dot_general | solution.py:42
  90.1 1.9 %copy-done.1 = f32[4,8,256,128]{3,2,1,0:T(8,128)} copy-done((f32[4,8,256,128]{3,2,1,0:T(8,128)}, f32[4,8,256,128]{3,2,1,0:T(8,128)S(1)}, u32[]{:S(2)}) %copy-start.1) | copy-done | bytes 4194328 | tf_op jit(solution)/shard_map/while
  92.0 2.9 %fusion.30 = bf16[256,4,8,128]{3,0,2,1:T(8,128)(2,1)S(1)} fusion(f32[4,8,256,128]{3,2,1,0:T(8,128)} %get-tuple-element.190, f32[4,8,256]{2,1,0:T(8,128)S(1)} %get-tuple-element.191), kind=kLoop, calls=%fused_computation.39 | loop fusion | flops 2097152 | bytes 6324224 | tf_op jit(solution)/shard_map/convert_element_type | solution.py:71
  94.9 2.7 %copy.30 = bf16[256,4,8,128]{3,2,1,0:T(8,128)(2,1)} copy(bf16[256,4,8,128]{3,0,2,1:T(8,128)(2,1)S(1)} %fusion.30) | data formatting | bytes 4194304 | tf_op jit(solution)/shard_map/convert_element_type | solution.py:71
  (63 shorter events, 17.9 us)
Async XLA Ops:
  5.7 2.2 %copy-start.3 = (bf16[256,4,128]{2,1,0:T(4,128)(2,1)S(1)}, bf16[256,4,128]{2,1,0:T(4,128)(2,1)}, u32[]{:S(2)}) copy-start(bf16[256,4,128]{2,1,0:T(4,128)(2,1)} %param.8) | copy-start | bytes 786436
  7.9 4.8 %copy-start.2 = (bf16[256,4,128]{2,1,0:T(4,128)(2,1)S(1)}, bf16[256,4,128]{2,1,0:T(4,128)(2,1)}, u32[]{:S(2)}) copy-start(bf16[256,4,128]{2,1,0:T(4,128)(2,1)} %param.7) | copy-start | bytes 786436
  7.9 4.9 %copy-start.4 = (s32[256]{0:T(256)S(1)}, s32[256]{0:T(256)}, u32[]{:S(2)}) copy-start(s32[256]{0:T(256)} %param.9) | copy-start | bytes 3076
  12.8 10.5 %collective-permute-start = (s32[256]{0:T(256)S(1)}, s32[256]{0:T(256)S(1)}, u32[]{:S(2)}, u32[]{:S(2)}) collective-permute-start(s32[256]{0:T(256)S(1)} %get-tuple-element.358), channel_id=1, source_target_pairs={{0,2},{2,4},{4,6},{6,8},{8,10},{10,12},{12,14},{14,16},{16,18},{18... | collective-permute-start | bytes 3080 | tf_op jit(solution)/shard_map/while/body/eval_jaxpr/ppermute | solution.py:12
  16.3 14.7 %collective-permute-start.1 = (bf16[256,4,128]{2,0,1:T(8,128)(2,1)S(1)}, bf16[256,4,128]{2,0,1:T(8,128)(2,1)S(1)}, u32[]{:S(2)}, u32[]{:S(2)}) collective-permute-start(bf16[256,4,128]{2,0,1:T(8,128)(2,1)S(1)} %get-tuple-element.356), channel_id=1, source_target_pairs={{0,2},{2,4},{4,6},{6,8},{8,10},{10,12},{12,14},{14,16},{16,18},{18... | collective-permute-start | bytes 786440 | tf_op jit(solution)/shard_map/while/body/eval_jaxpr/ppermute | solution.py:12
  19.8 15.4 %collective-permute-start.2 = (bf16[256,4,128]{2,0,1:T(8,128)(2,1)S(1)}, bf16[256,4,128]{2,0,1:T(8,128)(2,1)S(1)}, u32[]{:S(2)}, u32[]{:S(2)}) collective-permute-start(bf16[256,4,128]{2,0,1:T(8,128)(2,1)S(1)} %get-tuple-element.357), channel_id=1, source_target_pairs={{0,2},{2,4},{4,6},{6,8},{8,10},{10,12},{12,14},{14,16},{16,18},{18... | collective-permute-start | bytes 786440 | tf_op jit(solution)/shard_map/while/body/eval_jaxpr/ppermute | solution.py:12
  31.0 4.2 %copy-start = (f32[4,8,256,128]{3,2,1,0:T(8,128)S(1)}, f32[4,8,256,128]{3,2,1,0:T(8,128)}, u32[]{:S(2)}) copy-start(f32[4,8,256,128]{3,2,1,0:T(8,128)} %get-tuple-element.355) | copy-start | bytes 12582916 | tf_op jit(solution)/shard_map/while
  39.0 1.9 %copy-start.1 = (f32[4,8,256,128]{3,2,1,0:T(8,128)}, f32[4,8,256,128]{3,2,1,0:T(8,128)S(1)}, u32[]{:S(2)}) copy-start(f32[4,8,256,128]{3,2,1,0:T(8,128)S(1)} %multiply_add_fusion.5) | copy-start | bytes 12582916 | tf_op jit(solution)/shard_map/while
  40.9 9.1 %collective-permute-start = (s32[256]{0:T(256)S(1)}, s32[256]{0:T(256)S(1)}, u32[]{:S(2)}, u32[]{:S(2)}) collective-permute-start(s32[256]{0:T(256)S(1)} %get-tuple-element.358), channel_id=1, source_target_pairs={{0,2},{2,4},{4,6},{6,8},{8,10},{10,12},{12,14},{14,16},{16,18},{18... | collective-permute-start | bytes 3080 | tf_op jit(solution)/shard_map/while/body/eval_jaxpr/ppermute | solution.py:12
  42.8 14.7 %collective-permute-start.1 = (bf16[256,4,128]{2,0,1:T(8,128)(2,1)S(1)}, bf16[256,4,128]{2,0,1:T(8,128)(2,1)S(1)}, u32[]{:S(2)}, u32[]{:S(2)}) collective-permute-start(bf16[256,4,128]{2,0,1:T(8,128)(2,1)S(1)} %get-tuple-element.356), channel_id=1, source_target_pairs={{0,2},{2,4},{4,6},{6,8},{8,10},{10,12},{12,14},{14,16},{16,18},{18... | collective-permute-start | bytes 786440 | tf_op jit(solution)/shard_map/while/body/eval_jaxpr/ppermute | solution.py:12
  44.8 16.4 %collective-permute-start.2 = (bf16[256,4,128]{2,0,1:T(8,128)(2,1)S(1)}, bf16[256,4,128]{2,0,1:T(8,128)(2,1)S(1)}, u32[]{:S(2)}, u32[]{:S(2)}) collective-permute-start(bf16[256,4,128]{2,0,1:T(8,128)(2,1)S(1)} %get-tuple-element.357), channel_id=1, source_target_pairs={{0,2},{2,4},{4,6},{6,8},{8,10},{10,12},{12,14},{14,16},{16,18},{18... | collective-permute-start | bytes 786440 | tf_op jit(solution)/shard_map/while/body/eval_jaxpr/ppermute | solution.py:12
  57.6 3.6 %copy-start = (f32[4,8,256,128]{3,2,1,0:T(8,128)S(1)}, f32[4,8,256,128]{3,2,1,0:T(8,128)}, u32[]{:S(2)}) copy-start(f32[4,8,256,128]{3,2,1,0:T(8,128)} %get-tuple-element.355) | copy-start | bytes 12582916 | tf_op jit(solution)/shard_map/while
  64.9 1.9 %copy-start.1 = (f32[4,8,256,128]{3,2,1,0:T(8,128)}, f32[4,8,256,128]{3,2,1,0:T(8,128)S(1)}, u32[]{:S(2)}) copy-start(f32[4,8,256,128]{3,2,1,0:T(8,128)S(1)} %multiply_add_fusion.5) | copy-start | bytes 12582916 | tf_op jit(solution)/shard_map/while
  66.9 9.1 %collective-permute-start = (s32[256]{0:T(256)S(1)}, s32[256]{0:T(256)S(1)}, u32[]{:S(2)}, u32[]{:S(2)}) collective-permute-start(s32[256]{0:T(256)S(1)} %get-tuple-element.358), channel_id=1, source_target_pairs={{0,2},{2,4},{4,6},{6,8},{8,10},{10,12},{12,14},{14,16},{16,18},{18... | collective-permute-start | bytes 3080 | tf_op jit(solution)/shard_map/while/body/eval_jaxpr/ppermute | solution.py:12
  68.8 13.9 %collective-permute-start.1 = (bf16[256,4,128]{2,0,1:T(8,128)(2,1)S(1)}, bf16[256,4,128]{2,0,1:T(8,128)(2,1)S(1)}, u32[]{:S(2)}, u32[]{:S(2)}) collective-permute-start(bf16[256,4,128]{2,0,1:T(8,128)(2,1)S(1)} %get-tuple-element.356), channel_id=1, source_target_pairs={{0,2},{2,4},{4,6},{6,8},{8,10},{10,12},{12,14},{14,16},{16,18},{18... | collective-permute-start | bytes 786440 | tf_op jit(solution)/shard_map/while/body/eval_jaxpr/ppermute | solution.py:12
  70.7 15.6 %collective-permute-start.2 = (bf16[256,4,128]{2,0,1:T(8,128)(2,1)S(1)}, bf16[256,4,128]{2,0,1:T(8,128)(2,1)S(1)}, u32[]{:S(2)}, u32[]{:S(2)}) collective-permute-start(bf16[256,4,128]{2,0,1:T(8,128)(2,1)S(1)} %get-tuple-element.357), channel_id=1, source_target_pairs={{0,2},{2,4},{4,6},{6,8},{8,10},{10,12},{12,14},{14,16},{16,18},{18... | collective-permute-start | bytes 786440 | tf_op jit(solution)/shard_map/while/body/eval_jaxpr/ppermute | solution.py:12
  82.7 3.6 %copy-start = (f32[4,8,256,128]{3,2,1,0:T(8,128)S(1)}, f32[4,8,256,128]{3,2,1,0:T(8,128)}, u32[]{:S(2)}) copy-start(f32[4,8,256,128]{3,2,1,0:T(8,128)} %get-tuple-element.355) | copy-start | bytes 12582916 | tf_op jit(solution)/shard_map/while
  90.1 1.9 %copy-start.1 = (f32[4,8,256,128]{3,2,1,0:T(8,128)}, f32[4,8,256,128]{3,2,1,0:T(8,128)S(1)}, u32[]{:S(2)}) copy-start(f32[4,8,256,128]{3,2,1,0:T(8,128)S(1)} %multiply_add_fusion.5) | copy-start | bytes 12582916 | tf_op jit(solution)/shard_map/while
where the time goes:
time: 97.9 us; the launch traced here: 97.6 us
  waiting for transfers between devices  26.6 us (27%)
  starting transfers between devices  24 us (25%)
  matrix products  22.4 us (23%)
  other arithmetic  12.9 us (13%)
  local copies, waits for them, and re-layouts  11.1 us (11%)
    ppermute x9, waiting for transfers between devices, passed_along(): return lax.ppermute(x, axis, pairs)  26.6 us
    ppermute x9, starting transfers between devices, passed_along(): return lax.ppermute(x, axis, pairs)  24 us
    dot_general x4, matrix products, attend(): jnp.einsum('kgqs,skd->kgqd', weights.astype(jnp.bfloat16), val_tile, pref...  16.1 us
    reduce_sum x4, other arithmetic, attend(): new_sum = run_sum * rescale + jnp.sum(weights, axis=-1)  8.49 us
    dot_general x4, matrix products, attend(): jnp.einsum('qkgd,skd->kgqs', grouped, key_tile, preferred_element_type=jn...  6.37 us
    while x24, local copies, waits for them, and re-layouts  5.92 us
    convert_element_type x1, other arithmetic, local(): return result.transpose(2, 0, 1, 3).reshape(tok_rows, kv_local * group_si...  2.85 us
    convert_element_type x1, local copies, waits for them, and re-layouts, local(): return result.transpose(2, 0, 1, 3).reshape(tok_rows, kv_local * group_si...  2.67 us
  transfers between devices with their start and end apart: 9, of which 6 were waited for; matrix products, arithmetic and copies ran while one was open for 11% of the time, Pallas kernels for 0%

commit v1 on v0

v1 whole, which is shorter than its diff:
```python
import functools

import jax
import jax.numpy as jnp
from jax import lax
from jax.experimental import pallas as pl
from jax.experimental.pallas import tpu as pltpu
from jax.sharding import PartitionSpec as P

STEPS = 3
CHUNKS = 2
TOK_BLOCK = 64
SUB_ROWS = 256
MASKED = -1e30
LOG2E = 1.4426950408889634


def kernel(
    count, ctx, tok, kv, group, head_dim,
    q_hbm, k_hbm, v_hbm, seg_hbm, o_hbm,
    q_in, held, seg, plain, key_t, val_t, q_t, bias, top, total, acc, out,
    send_sem, recv_sem, seg_send, seg_recv, local_sem, out_sem,
):
    me = lax.axis_index("dcn") * ctx + lax.axis_index("ctx")

    def device(position):
        return {"dcn": position // ctx, "ctx": position % ctx}

    right = lax.rem(me + 1, count)
    left = lax.rem(me + count - 1, count)
    has_right = me < count - 1

    half = tok // CHUNKS

    def pass_chunk(d, which, c):
        rows = pl.ds(c * half * kv, half * kv)
        source = (k_hbm, v_hbm)[which].at[rows] if d == 0 else held.at[d, which, rows]
        return pltpu.make_async_remote_copy(
            src_ref=source,
            dst_ref=held.at[d + 1, which, rows],
            send_sem=send_sem.at[d, which, c],
            recv_sem=recv_sem.at[d, which, c],
            device_id=device(right),
            device_id_type=pl.DeviceIdType.MESH,
        )

    def pass_seg(d):
        return pltpu.make_async_remote_copy(
            src_ref=seg_hbm if d == 0 else seg.at[d],
            dst_ref=seg.at[d + 1],
            send_sem=seg_send.at[d],
            recv_sem=seg_recv.at[d],
            device_id=device(right),
            device_id_type=pl.DeviceIdType.MESH,
        )

    loads = [
        pltpu.make_async_copy(seg_hbm, seg.at[0], local_sem.at[0]),
        pltpu.make_async_copy(k_hbm, held.at[0, 0], local_sem.at[1]),
        pltpu.make_async_copy(v_hbm, held.at[0, 1], local_sem.at[2]),
        pltpu.make_async_copy(q_hbm, q_in, local_sem.at[3]),
    ]
    for load in loads:
        load.start()

    barrier = pltpu.get_barrier_semaphore()
    for neighbour in (left, right):
        pl.semaphore_signal(
            barrier, inc=1, device_id=device(neighbour), device_id_type=pl.DeviceIdType.MESH
        )
    pl.semaphore_wait(barrier, 2)

    order = [(c, which) for c in reversed(range(CHUNKS)) for which in range(2)]

    @pl.when(has_right)
    def _():
        pass_seg(0).start()
        for c, which in order:
            pass_chunk(0, which, c).start()

    for load in loads:
        load.wait()

    def split_queries(block, carry):
        tokens = pl.ds(pl.multiple_of(block * TOK_BLOCK, TOK_BLOCK), TOK_BLOCK)
        rows = pl.ds(pl.multiple_of(block * TOK_BLOCK * group, TOK_BLOCK * group), TOK_BLOCK * group)
        for pair in range(kv // 2):
            both = q_in[tokens, pl.ds(pair * 2 * group, 2 * group), :].astype(jnp.float32)
            for i in range(2):
                one = both[:, i * group:(i + 1) * group, :]
                q_t[2 * pair + i, rows, :] = one.reshape(TOK_BLOCK * group, head_dim).astype(jnp.bfloat16)
        return carry

    lax.fori_loop(0, tok // TOK_BLOCK, split_queries, 0)

    own_row = seg[0].astype(jnp.float32)
    at_row = lax.broadcasted_iota(jnp.int32, (tok, tok), 0)
    at_col = lax.broadcasted_iota(jnp.int32, (tok, tok), 1)
    own_col = jnp.sum(jnp.where(at_row == at_col, own_row, 0.0), axis=1, keepdims=True)

    def set_bias(d):
        ok = own_col == seg[d].astype(jnp.float32)
        if d == 0:
            ok = ok & (at_col <= at_row)
        one = jnp.where(ok, 0.0, MASKED)
        bias[...] = jnp.broadcast_to(one[:, None, :], (tok, group, tok)).reshape(tok * group, tok)

    def split_heads(d, key0, keys):
        rows = pl.ds(key0 * kv, keys * kv)
        for which, dest in ((0, key_t), (1, val_t)):
            plain[which, rows, :] = held[d, which, rows, :].astype(jnp.float32)
            for g in range(kv):
                dest[g, pl.ds(key0, keys), :] = plain[
                    which, pl.ds(key0 * kv + g, keys, stride=kv), :
                ].astype(jnp.bfloat16)

    factor = head_dim ** (-0.5) * LOG2E

    def attend(key0, keys, tokens, first):
        blocks = tokens // TOK_BLOCK
        span = TOK_BLOCK * group
        parts = keys // 128

        def body(step, carry):
            g = step // blocks
            base = (step % blocks) * span
            k = key_t[g, pl.ds(key0, keys), :]
            v = val_t[g, pl.ds(key0, keys), :]
            for sub in range(span // SUB_ROWS):
                rows = pl.ds(pl.multiple_of(base + sub * SUB_ROWS, SUB_ROWS), SUB_ROWS)
                s = lax.dot_general(
                    q_t[g, rows, :], k, (((1,), (1,)), ((), ())),
                    preferred_element_type=jnp.float32,
                )
                s = s * factor + bias[rows, pl.ds(key0, keys)]
                high = jnp.broadcast_to(jnp.max(s, axis=1, keepdims=True), (SUB_ROWS, 128))
                if not first:
                    before = top[g, rows, :]
                    high = jnp.maximum(high, before)
                weights = [jnp.exp2(s[:, i * 128:(i + 1) * 128] - high) for i in range(parts)]
                summed = functools.reduce(jnp.add, weights)
                w = jnp.concatenate([x.astype(jnp.bfloat16) for x in weights], axis=1)
                update = jnp.dot(w, v, preferred_element_type=jnp.float32)
                if not first:
                    rescale = jnp.exp2(before - high)
                    summed = summed + total[g, rows, :] * rescale
                    update = update + acc[g, rows, :] * rescale
                top[g, rows, :] = high
                total[g, rows, :] = summed
                acc[g, rows, :] = update
            return carry

        lax.fori_loop(0, kv * blocks, body, 0)

    set_bias(0)
    split_heads(0, 0, tok)
    attend(0, tok, tok, True)

    for d in range(1, STEPS + 1):
        @pl.when(me >= d)
        def _(d=d):
            pass_seg(d - 1).wait_recv()
            if d < STEPS:
                @pl.when(has_right)
                def _():
                    pass_seg(d).start()
            set_bias(d)
            for c in reversed(range(CHUNKS)):
                for which in range(2):
                    pass_chunk(d - 1, which, c).wait_recv()
                    if d < STEPS:
                        @pl.when(has_right)
                        def _(which=which, c=c):
                            pass_chunk(d, which, c).start()
                if d == STEPS:
                    split_heads(d, c * half, half)
                    attend(c * half, half, (c + 1) * half, False)
            if d < STEPS:
                split_heads(d, 0, tok)
                attend(0, tok, tok, False)

    def finish(block, carry):
        tokens = pl.ds(pl.multiple_of(block * TOK_BLOCK, TOK_BLOCK), TOK_BLOCK)
        rows = pl.ds(pl.multiple_of(block * TOK_BLOCK * group, TOK_BLOCK * group), TOK_BLOCK * group)
        for pair in range(kv // 2):
            done = []
            for i in range(2):
                g = 2 * pair + i
                whole = jnp.sum(total[g, rows, :], axis=1, keepdims=True)
                done.append((acc[g, rows, :] / whole).reshape(TOK_BLOCK, group, head_dim))
            out[tokens, pl.ds(pair * 2 * group, 2 * group), :] = jnp.concatenate(done, axis=1).astype(jnp.bfloat16)
        return carry

    lax.fori_loop(0, tok // TOK_BLOCK, finish, 0)
    write = pltpu.make_async_copy(out, o_hbm, out_sem)
    write.start()

    for d in range(STEPS):
        @pl.when(has_right & (me >= d))
        def _(d=d):
            pass_seg(d).wait_send()
            for c, which in order:
                pass_chunk(d, which, c).wait_send()
    write.wait()


def local(queries, keys, values, seg_ids):
    tok, heads, head_dim = queries.shape
    kv = keys.shape[1]
    group = heads // kv
    ctx = lax.axis_size("ctx")
    count = lax.axis_size("dcn") * ctx
    rows = tok * group
    bf16, f32 = jnp.bfloat16, jnp.float32
    return pl.pallas_call(
        functools.partial(kernel, count, ctx, tok, kv, group, head_dim),
        out_shape=jax.ShapeDtypeStruct((tok, heads, head_dim), bf16),
        in_specs=[pl.BlockSpec(memory_space=pltpu.HBM)] * 4,
        out_specs=pl.BlockSpec(memory_space=pltpu.HBM),
        scratch_shapes=[
            pltpu.VMEM((tok, heads, head_dim), bf16),
            pltpu.VMEM((STEPS + 1, 2, tok * kv, head_dim), bf16),
            pltpu.VMEM((STEPS + 1, 1, tok), jnp.int32),
            pltpu.VMEM((2, tok * kv, head_dim), f32),
            pltpu.VMEM((kv, tok, head_dim), bf16),
            pltpu.VMEM((kv, tok, head_dim), bf16),
            pltpu.VMEM((kv, rows, head_dim), bf16),
            pltpu.VMEM((rows, tok), f32),
            pltpu.VMEM((kv, rows, 128), f32),
            pltpu.VMEM((kv, rows, 128), f32),
            pltpu.VMEM((kv, rows, head_dim), f32),
            pltpu.VMEM((tok, heads, head_dim), bf16),
            pltpu.SemaphoreType.DMA((STEPS, 2, CHUNKS)),
            pltpu.SemaphoreType.DMA((STEPS, 2, CHUNKS)),
            pltpu.SemaphoreType.DMA((STEPS,)),
            pltpu.SemaphoreType.DMA((STEPS,)),
            pltpu.SemaphoreType.DMA((4,)),
            pltpu.SemaphoreType.DMA,
        ],
        compiler_params=pltpu.CompilerParams(
            collective_id=0, has_side_effects=True, vmem_limit_bytes=56 * 1024 * 1024
        ),
    )(
        queries,
        keys.reshape(tok * kv, head_dim),
        values.reshape(tok * kv, head_dim),
        seg_ids.reshape(1, tok),
    )


def solution(mesh):
    placed = (
        P(("dcn", "ctx"), "head", None),
        P(("dcn", "ctx"), "head", None),
        P(("dcn", "ctx"), "head", None),
        P(("dcn", "ctx")),
    )
    return jax.shard_map(
        local,
        mesh=mesh,
        in_specs=placed,
        out_specs=P(("dcn", "ctx"), "head", None),
        check_vma=False,
    )
```

time: 97.9 us -> 63.4 us (0.65)
  Pallas kernels: 0 us -> 60 us
  waiting for transfers between devices: 26.6 us -> 0 us
  starting transfers between devices: 24 us -> 0 us
  matrix products: 22.4 us -> 0 us
  other arithmetic: 12.9 us -> 0 us
  local copies, waits for them, and re-layouts: 11.1 us -> 3.27 us
    pallas_call x0 -> x1, Pallas kernels: none -> 60 us  [local(): pl.pallas_call(functools.partial(kernel, count, ctx, tok, kv, group, head...]
    ppermute x9 -> x0, waiting for transfers between devices: 26.6 us -> none  [passed_along(): return lax.ppermute(x, axis, pairs)]
    ppermute x9 -> x0, starting transfers between devices: 24 us -> none  [passed_along(): return lax.ppermute(x, axis, pairs)]
    dot_general x8 -> x0, matrix products: 22.4 us -> none  [the longest x4 16.1 us: attend(): jnp.einsum('kgqs,skd->kgqd', weights.astype(jnp.bfloat16), val_tile, pref...]
    reduce_sum x4 -> x0, other arithmetic: 8.49 us -> none  [attend(): new_sum = run_sum * rescale + jnp.sum(weights, axis=-1)]
    while x24 -> x0, local copies, waits for them, and re-layouts: 5.92 us -> none
    convert_element_type x1 -> x0, other arithmetic: 2.85 us -> none  [local(): return result.transpose(2, 0, 1, 3).reshape(tok_rows, kv_local * group_si...]
    convert_element_type x1 -> x0, local copies, waits for them, and re-layouts: 2.67 us -> none  [local(): return result.transpose(2, 0, 1, 3).reshape(tok_rows, kv_local * group_si...]
  transfers between devices with their start and end apart: 9 -> 0, of which waited for: 6 -> 0; matrix products, arithmetic and copies ran while one was open for 11% -> 0% of each run, Pallas kernels for 0% -> 0%
where the time goes in v1:
time: 63.4 us; the launch traced here: 63.3 us
  Pallas kernels  60 us (95%)
  local copies, waits for them, and re-layouts  3.27 us (5%)
    pallas_call x1, Pallas kernels, local(): pl.pallas_call(functools.partial(kernel, count, ctx, tok, kv, group, head...  60 us
    unnamed x1, local copies, waits for them, and re-layouts  3.27 us

profile of v1, /device:TPU:4, one launch (start us, length us, event | category | flops | bytes accessed | tf_op | source)
XLA Modules:
  0.0 63.3 jit_solution(15177953370722330321)
XLA Ops:
  0.0 60.0 %shard_map.46 = bf16[256,32,128]{2,1,0:T(8,128)(2,1)} custom-call(bf16[256,32,128]{2,1,0:T(8,128)(2,1)} %q_hbm.1, bf16[1024,128]{1,0:T(8,128)(2,1)} %bitcast.3, bf16[1024,128]{1,0:T(8,128)(2,1)} %bitcast.4, s32[1,256]{1,0:T(1,128)} %bitcast.5), custom_call_target="tpu_custom_call" | custom-call | tf_op jit(solution)/shard_map/pallas_call | solution.py:215
  60.0 3.3 %copy.6 = bf16[256,32,128]{2,1,0:T(8,128)(2,1)} copy(bf16[256,32,128]{2,1,0:T(8,128)(2,1)} %shard_map.46) | data formatting | bytes 4194304

commit v2 on v1

--- a/solution.py
+++ b/solution.py
@@ -9,7 +9,8 @@
 
 STEPS = 3
 CHUNKS = 2
-TOK_BLOCK = 64
+TOK_BLOCK = 128
+PART = 32
 SUB_ROWS = 256
 MASKED = -1e30
 LOG2E = 1.4426950408889634
@@ -126,8 +127,12 @@
             base = (step % blocks) * span
             k = key_t[g, pl.ds(key0, keys), :]
             v = val_t[g, pl.ds(key0, keys), :]
-            for sub in range(span // SUB_ROWS):
-                rows = pl.ds(pl.multiple_of(base + sub * SUB_ROWS, SUB_ROWS), SUB_ROWS)
+            spans = [
+                pl.ds(pl.multiple_of(base + sub * SUB_ROWS, SUB_ROWS), SUB_ROWS)
+                for sub in range(span // SUB_ROWS)
+            ]
+            results = []
+            for rows in spans:
                 s = lax.dot_general(
                     q_t[g, rows, :], k, (((1,), (1,)), ((), ())),
                     preferred_element_type=jnp.float32,
@@ -145,6 +150,8 @@
                     rescale = jnp.exp2(before - high)
                     summed = summed + total[g, rows, :] * rescale
                     update = update + acc[g, rows, :] * rescale
+                results.append((high, summed, update))
+            for rows, (high, summed, update) in zip(spans, results):
                 top[g, rows, :] = high
                 total[g, rows, :] = summed
                 acc[g, rows, :] = update
@@ -155,6 +162,14 @@
     set_bias(0)
     split_heads(0, 0, tok)
     attend(0, tok, tok, True)
+
+    def receive(d, c):
+        for which in range(2):
+            pass_chunk(d - 1, which, c).wait_recv()
+            if d < STEPS:
+                @pl.when(has_right)
+                def _(which=which):
+                    pass_chunk(d, which, c).start()
 
     for d in range(1, STEPS + 1):
         @pl.when(me >= d)
@@ -165,35 +180,42 @@
                 def _():
                     pass_seg(d).start()
             set_bias(d)
-            for c in reversed(range(CHUNKS)):
-                for which in range(2):
-                    pass_chunk(d - 1, which, c).wait_recv()
-                    if d < STEPS:
-                        @pl.when(has_right)
-                        def _(which=which, c=c):
-                            pass_chunk(d, which, c).start()
-                if d == STEPS:
-                    split_heads(d, c * half, half)
-                    attend(c * half, half, (c + 1) * half, False)
             if d < STEPS:
+                for c in reversed(range(CHUNKS)):
+                    receive(d, c)
                 split_heads(d, 0, tok)
                 attend(0, tok, tok, False)
 
-    def finish(block, carry):
-        tokens = pl.ds(pl.multiple_of(block * TOK_BLOCK, TOK_BLOCK), TOK_BLOCK)
-        rows = pl.ds(pl.multiple_of(block * TOK_BLOCK * group, TOK_BLOCK * group), TOK_BLOCK * group)
-        for pair in range(kv // 2):
-            done = []
-            for i in range(2):
-                g = 2 * pair + i
-                whole = jnp.sum(total[g, rows, :], axis=1, keepdims=True)
-                done.append((acc[g, rows, :] / whole).reshape(TOK_BLOCK, group, head_dim))
-            out[tokens, pl.ds(pair * 2 * group, 2 * group), :] = jnp.concatenate(done, axis=1).astype(jnp.bfloat16)
-        return carry
-
-    lax.fori_loop(0, tok // TOK_BLOCK, finish, 0)
-    write = pltpu.make_async_copy(out, o_hbm, out_sem)
-    write.start()
+    def finish(first_block, blocks):
+        def body(block, carry):
+            tokens = pl.ds(pl.multiple_of(block * PART, PART), PART)
+            rows = pl.ds(pl.multiple_of(block * PART * group, PART * group), PART * group)
+            for pair in range(kv // 2):
+                done = []
+                for i in range(2):
+                    g = 2 * pair + i
+                    whole = jnp.sum(total[g, rows, :], axis=1, keepdims=True)
+                    done.append((acc[g, rows, :] / whole).reshape(PART, group, head_dim))
+                out[tokens, pl.ds(pair * 2 * group, 2 * group), :] = (
+                    jnp.concatenate(done, axis=1).astype(jnp.bfloat16)
+                )
+            return carry
+
+        lax.fori_loop(first_block, first_block + blocks, body, 0)
+
+    def write(c):
+        tokens = pl.ds(c * half, half)
+        return pltpu.make_async_copy(out.at[tokens], o_hbm.at[tokens], out_sem.at[c])
+
+    for c in reversed(range(CHUNKS)):
+        @pl.when(me >= STEPS)
+        def _(c=c):
+            receive(STEPS, c)
+            split_heads(STEPS, c * half, half)
+            attend(c * half, half, (c + 1) * half, False)
+
+        finish(c * half // PART, half // PART)
+        write(c).start()
 
     for d in range(STEPS):
         @pl.when(has_right & (me >= d))
@@ -201,7 +223,8 @@
             pass_seg(d).wait_send()
             for c, which in order:
                 pass_chunk(d, which, c).wait_send()
-    write.wait()
+    for c in range(CHUNKS):
+        write(c).wait()
 
 
 def local(queries, keys, values, seg_ids):
@@ -235,7 +258,7 @@
             pltpu.SemaphoreType.DMA((STEPS,)),
             pltpu.SemaphoreType.DMA((STEPS,)),
             pltpu.SemaphoreType.DMA((4,)),
-            pltpu.SemaphoreType.DMA,
+            pltpu.SemaphoreType.DMA((CHUNKS,)),
         ],
         compiler_params=pltpu.CompilerParams(
             collective_id=0, has_side_effects=True, vmem_limit_bytes=56 * 1024 * 1024

time: 63.4 us -> 52 us (0.82)
  Pallas kernels: 60 us -> 48.6 us
    pallas_call x1, Pallas kernels: 60 us -> 48.6 us  [local(): pl.pallas_call(functools.partial(kernel, count, ctx, tok, kv, group, head...]
where the time goes in v2:
time: 52 us; the launch traced here: 51.9 us
  Pallas kernels  48.6 us (93%)
  local copies, waits for them, and re-layouts  3.27 us (6%)
    pallas_call x1, Pallas kernels, local(): pl.pallas_call(functools.partial(kernel, count, ctx, tok, kv, group, head...  48.6 us
    unnamed x1, local copies, waits for them, and re-layouts  3.27 us

profile of v2, /device:TPU:4, one launch (start us, length us, event | category | flops | bytes accessed | tf_op | source)
XLA Modules:
  0.0 51.9 jit_solution(7652405465697205681)
XLA Ops:
  0.0 48.6 %shard_map.46 = bf16[256,32,128]{2,1,0:T(8,128)(2,1)} custom-call(bf16[256,32,128]{2,1,0:T(8,128)(2,1)} %q_hbm.1, bf16[1024,128]{1,0:T(8,128)(2,1)} %bitcast.3, bf16[1024,128]{1,0:T(8,128)(2,1)} %bitcast.4, s32[1,256]{1,0:T(1,128)} %bitcast.5), custom_call_target="tpu_custom_call" | custom-call | tf_op jit(solution)/shard_map/pallas_call | solution.py:238
  48.6 3.3 %copy.6 = bf16[256,32,128]{2,1,0:T(8,128)(2,1)} copy(bf16[256,32,128]{2,1,0:T(8,128)(2,1)} %shard_map.46) | data formatting | bytes 4194304

commit v3 on v2

--- a/solution.py
+++ b/solution.py
@@ -9,7 +9,7 @@
 
 STEPS = 3
 CHUNKS = 2
-TOK_BLOCK = 128
+TOK_BLOCK = 256
 PART = 32
 SUB_ROWS = 256
 MASKED = -1e30
@@ -83,16 +83,16 @@
         load.wait()
 
     def split_queries(block, carry):
-        tokens = pl.ds(pl.multiple_of(block * TOK_BLOCK, TOK_BLOCK), TOK_BLOCK)
-        rows = pl.ds(pl.multiple_of(block * TOK_BLOCK * group, TOK_BLOCK * group), TOK_BLOCK * group)
+        tokens = pl.ds(pl.multiple_of(block * PART, PART), PART)
+        rows = pl.ds(pl.multiple_of(block * PART * group, PART * group), PART * group)
         for pair in range(kv // 2):
             both = q_in[tokens, pl.ds(pair * 2 * group, 2 * group), :].astype(jnp.float32)
             for i in range(2):
                 one = both[:, i * group:(i + 1) * group, :]
-                q_t[2 * pair + i, rows, :] = one.reshape(TOK_BLOCK * group, head_dim).astype(jnp.bfloat16)
+                q_t[2 * pair + i, rows, :] = one.reshape(PART * group, head_dim).astype(jnp.bfloat16)
         return carry
 
-    lax.fori_loop(0, tok // TOK_BLOCK, split_queries, 0)
+    lax.fori_loop(0, tok // PART, split_queries, 0)
 
     own_row = seg[0].astype(jnp.float32)
     at_row = lax.broadcasted_iota(jnp.int32, (tok, tok), 0)
@@ -118,8 +118,9 @@
     factor = head_dim ** (-0.5) * LOG2E
 
     def attend(key0, keys, tokens, first):
-        blocks = tokens // TOK_BLOCK
-        span = TOK_BLOCK * group
+        at_once = min(tokens, TOK_BLOCK)
+        blocks = tokens // at_once
+        span = at_once * group
         parts = keys // 128
 
         def body(step, carry):

time: 52 us -> 48.9 us (0.940)
  Pallas kernels: 48.6 us -> 45.4 us
    pallas_call x1, Pallas kernels: 48.6 us -> 45.4 us  [local(): pl.pallas_call(functools.partial(kernel, count, ctx, tok, kv, group, head...]
where the time goes in v3:
time: 48.9 us; the launch traced here: 48.7 us
  Pallas kernels  45.4 us (93%)
  local copies, waits for them, and re-layouts  3.27 us (7%)
    pallas_call x1, Pallas kernels, local(): pl.pallas_call(functools.partial(kernel, count, ctx, tok, kv, group, head...  45.4 us
    unnamed x1, local copies, waits for them, and re-layouts  3.27 us

profile of v3, /device:TPU:4, one launch (start us, length us, event | category | flops | bytes accessed | tf_op | source)
XLA Modules:
  0.0 48.7 jit_solution(8966269256775175338)
XLA Ops:
  0.0 45.4 %shard_map.46 = bf16[256,32,128]{2,1,0:T(8,128)(2,1)} custom-call(bf16[256,32,128]{2,1,0:T(8,128)(2,1)} %q_hbm.1, bf16[1024,128]{1,0:T(8,128)(2,1)} %bitcast.3, bf16[1024,128]{1,0:T(8,128)(2,1)} %bitcast.4, s32[1,256]{1,0:T(1,128)} %bitcast.5), custom_call_target="tpu_custom_call" | custom-call | tf_op jit(solution)/shard_map/pallas_call | solution.py:239
  45.4 3.3 %copy.6 = bf16[256,32,128]{2,1,0:T(8,128)(2,1)} copy(bf16[256,32,128]{2,1,0:T(8,128)(2,1)} %shard_map.46) | data formatting | bytes 4194304
